TPU v7x, 512 devices: a whole 4x8x8 slice. The times are simulated.
512 devices in a mesh: depth: 8 (over y), lat: 32 (over z, x), freq: 2 (over core).
Axes of the slice: x: 4, y: 8, z: 8, core: 2. Of those that a mesh axis runs over, the one named last changes fastest.
Arguments:
- surface: bfloat16 [6, 2, 128, 32768], P('freq', None, None, 'lat'), may hold values from -6 to 6
- refl: float32 [8, 32768], P('depth', 'lat'), may hold values from -0.5 to 0.5
- pool: bfloat16 [8, 6, 8, 128, 256], P('depth', 'freq'), may hold values from -0.375 to 0.375
- tile_ids: int32 [8, 256, 10], P('depth', 'lat'), may hold values from 0 to 255, as said below
- block_ids: int32 [8, 256, 10], P('depth', 'lat'), may hold values from 0 to 7
- counts: int32 [8, 256], P('depth', 'lat'), may hold values from 1 to 10, as said below
Outputs:
- image: float32 [8, 32768], P('depth', 'lat')
Inputs may be any that keep to these rules, and one draw needn't show every extreme that they name: tile_ids[l, j, k] = (j + o) mod 256 for an offset o with -8 <= o <= 8; slot 0 names the row's own tile; in every level some row has all 10 slots live with offsets 8 at slot 1 and -8 at slot 2. Slots k >= counts[l, j] of row j are padding; in every level some row has all 10 slots live.
All inputs are finite; a program needn't handle non-finite values.
Results may differ from a plain program's by a relative error of at most 0.00055.
Values may be sent and summed in bfloat16 or wider, within the bound.
A program may use at most 128 MiB of HBM per device.

v0:
```python
import jax
import jax.numpy as jnp
from jax import lax
from jax.sharding import PartitionSpec as P

TILE = 128
TILE_DEV = 8


def extended_2(block, sides, width):
    for axis, dim in sides:
        count = lax.axis_size(axis)
        forward = [(i, i + 1) for i in range(count - 1)]
        forward.append((count - 1, 0))
        backward = [(target, source) for source, target in forward]
        low = lax.ppermute(
            lax.slice_in_dim(block, block.shape[dim] - width, None, axis=dim), axis, forward
        )
        high = lax.ppermute(lax.slice_in_dim(block, 0, width, axis=dim), axis, backward)
        block = jnp.concatenate([low, block, high], axis=dim)
    return block


def in_one_piece(arrays, axis, dim, along):
    columns = [a.reshape(*a.shape[:along], -1) for a in arrays]
    both = jnp.concatenate(columns, axis=along)
    whole, at, gathered = (lax.all_gather(both, axis, axis=dim, tiled=True), 0, [])
    for a, column in zip(arrays, columns):
        piece = whole[..., at : at + column.shape[along]]
        gathered.append(piece.reshape(*piece.shape[:along], *a.shape[along:]))
        at += column.shape[along]
    return tuple(gathered)


def copy_for_each(shard, axis):
    copies = jnp.broadcast_to(shard, (lax.axis_size(axis), *shard.shape))
    return lax.all_to_all(copies, axis, split_axis=0, concat_axis=0, tiled=True)


def in_order(parts, dim):
    parts = jnp.moveaxis(parts, 0, dim)
    shape = parts.shape
    return parts.reshape(*shape[:dim], shape[dim] * shape[dim + 1], *shape[dim + 2 :])


def gather_directly(shard, axis, dim):
    parts = copy_for_each(shard, axis)
    return in_order(parts, dim)


def cut_along(shard, dim, length):
    before, after = (shard.shape[:dim], shard.shape[dim + 1 :])
    return jnp.moveaxis(shard.reshape(*before, length, -1, *after), dim, 0)


def summed_on_arrival(shard, axis, dim):
    parts = cut_along(shard, dim, lax.axis_size(axis))
    arrived = lax.all_to_all(parts, axis, split_axis=0, concat_axis=0, tiled=True)
    return arrived.sum(axis=0)


def aperture_rim(wave_field):
    return extended_2(wave_field, (("lat", 3),), TILE_DEV * TILE)


def extrapolate(extended, pool_level, local_ids, block_level, count_level, refl_level):
    freqs_here = extended.shape[0]
    shot_rows = extended.shape[2]
    tile_rows = local_ids.shape[0]
    slot_total = local_ids.shape[1]
    tile_grid = extended.reshape(freqs_here, 2, shot_rows, -1, TILE)
    slot_live = (jnp.arange(slot_total)[None, :] < count_level[:, None]).astype(jnp.bfloat16)
    picked = jnp.take(tile_grid, local_ids, axis=3) * slot_live[None, None, None, :, :, None]
    chosen = jnp.take(pool_level, block_level, axis=1)
    product = jnp.einsum("fsarkt,frktc->rfsac", picked, chosen, preferred_element_type=jnp.float32)
    real_part = product[:, :, 0, :, :TILE] - product[:, :, 1, :, TILE:]
    imag_part = product[:, :, 0, :, TILE:] + product[:, :, 1, :, :TILE]
    row_scale = 1.0 / jnp.sqrt(count_level.astype(jnp.float32))
    rows_out = jnp.stack([real_part, imag_part], 2) * row_scale[:, None, None, None, None]
    wave_out = jnp.transpose(rows_out, (1, 2, 3, 0, 4)).reshape(
        freqs_here, 2, shot_rows, tile_rows * TILE
    )
    wave_out = wave_out * (1.0 - refl_level)
    return (wave_out.astype(jnp.bfloat16), jnp.sum(wave_out * wave_out, axis=(0, 1, 2)))


def per_device(surface, refl, pool, tile_ids, block_ids, counts):
    depth_index = lax.axis_index("depth")
    lat_index = lax.axis_index("lat")
    tile_count = TILE_DEV * lax.axis_size("lat")
    first_tile = lat_index * TILE_DEV - TILE_DEV
    freqs_here = surface.shape[0]
    shot_total = surface.shape[2]
    lateral_width = surface.shape[3]
    shot_rows = shot_total // lax.axis_size("depth")
    own_shots = lax.dynamic_slice_in_dim(surface, depth_index * shot_rows, shot_rows, 2)
    pool_all = lax.all_gather(pool, "depth", axis=0, tiled=True)
    ids_all, blocks_all, counts_all = in_one_piece((tile_ids, block_ids, counts), "depth", 0, 2)
    refl_all = gather_directly(refl, "depth", 0)
    level_total = pool_all.shape[0]

    def level_step(level_index, loop_state):
        wave_field, images = loop_state
        ids_here = lax.dynamic_index_in_dim(ids_all, level_index, 0, keepdims=False)
        local_level = jnp.mod(ids_here - first_tile, tile_count)
        pool_here = lax.dynamic_index_in_dim(pool_all, level_index, 0, keepdims=False)
        blocks_here = lax.dynamic_index_in_dim(blocks_all, level_index, 0, keepdims=False)
        counts_here = lax.dynamic_index_in_dim(counts_all, level_index, 0, keepdims=False)
        refl_here = lax.dynamic_index_in_dim(refl_all, level_index, 0, keepdims=False)
        handed, partial_value = extrapolate(
            aperture_rim(wave_field), pool_here, local_level, blocks_here, counts_here, refl_here
        )
        images = lax.dynamic_update_index_in_dim(images, partial_value, level_index, 0)
        return (handed, images)

    start_images = jnp.zeros((level_total, lateral_width), jnp.float32)
    loop_state = lax.fori_loop(0, level_total, level_step, (own_shots, start_images))
    image_local = summed_on_arrival(loop_state[1], "depth", 0)[0]
    summed = lax.psum(image_local, "freq")
    divisor = freqs_here * lax.axis_size("freq") * shot_total
    return (summed / divisor)[None, :]


def solution(mesh):
    placed = (
        P("freq", None, None, "lat"),
        P("depth", "lat"),
        P("depth", "freq", None, None, None),
        P("depth", "lat", None),
        P("depth", "lat", None),
        P("depth", "lat"),
    )
    return jax.shard_map(
        per_device, mesh=mesh, in_specs=placed, out_specs=P("depth", "lat"), check_vma=False
    )
```

profile of v0, /device:TPU:1, one launch (start us, length us, event | category | flops | bytes accessed | tf_op | source)
XLA Modules:
  0.0 460.4 jit_solution(3497054629939524282)
XLA Ops:
  8.6 7.7 %all-to-all-start = ((f32[8,1,1024]{2,1,0:T(1,128)}), f32[8,1,1024]{2,1,0:T(1,128)S(1)}, u32[]{:S(2)}, u32[]{:S(2)}) async-start(f32[8,1,1024]{2,1,0:T(1,128)} %broadcast_in_dim.88), calls=%async_computation | async-start | bytes 65536 | tf_op jit(solution)/shard_map/all_to_all | solution.py:37
  17.7 20.8 %all_gather.6 = s32[8,8,21]{2,1,0:T(8,128)S(1)} all-gather(s32[1,8,21]{2,1,0:T(8,128)S(1)} %pad_add_fusion), channel_id=1, replica_groups=mesh['depth'=8,'lat'=32,'freq'=2] {'depth'}, dimensions={0}, use_global_device_ids=true | all-gather | bytes 6048 | tf_op jit(solution)/shard_map/all_gather | solution.py:27
  40.0 110.9 %all-gather.2.cloned.1.call-done = bf16[8,3,8,128,256]{4,3,2,1,0:T(8,128)(2,1)} async-done(((bf16[1,3,8,128,256]{4,3,2,1,0:T(8,128)(2,1)}), bf16[8,3,8,128,256]{4,3,2,1,0:T(8,128)(2,1)}) %all-gather.2.cloned.1.call-update) | async-done | bytes 12582928 | tf_op jit(solution)/shard_map/all_gather | solution.py:97
  150.9 281.9 %while.17 = (s32[]{:T(128)}, bf16[3,2,16,1024]{3,2,1,0:T(8,128)(2,1)S(1)}, f32[8,1024]{1,0:T(8,128)}, s32[8,8,10]{2,1,0:T(8,128)S(1)}, s32[]{:T(128)}, /*index=5...) while((s32[]{:T(128)}, ...), condition=%wide.region_2.3_spmd, body=%wide.region_0.2_spmd.sunk | while | flops 515904960 | bytes 62015692 | solution.py:117
  150.9 7.8 %collective-permute-start = (bf16[3,2,16,1024]{3,2,1,0:T(8,128)(2,1)S(1)}, bf16[3,2,16,1024]{3,2,1,0:T(8,128)(2,1)S(1)}, u32[]{:S(2)}, u32[]{:S(2)}) collective-permute-start(bf16[3,2,16,1024]{3,2,1,0:T(8,128)(2,1)S(1)} %get-tuple-element.365), channel_id=1, source_target_pairs={{2,0},{4,2},{6,4},{8,6},{10,8},{12,10},{14,12},{16,14},{18,16},{20... | collective-permute-start | bytes 589832 | tf_op jit(solution)/shard_map/while/body/eval_jaxpr/ppermute | solution.py:19
  164.9 8.1 %gather_fusion = bf16[80,3,128,256]{3,2,1,0:T(8,128)(2,1)} fusion(bf16[3,8,128,256]{3,2,1,0:T(8,128)(2,1)S(1)} %dynamic-slice_bitcast_fusion.2, s32[1024]{0:T(1024)S(1)} %pad_clamp_fusion.4), kind=kCustom, calls=%fused_computation.1.clone.1 | custom fusion | bytes 31457600 | tf_op jit(solution)/shard_map/while/body/eval_jaxpr/jit(_take)/gather | solution.py:74
  177.3 8.0 %fusion.30 = f32[8,3,2,16,256]{4,3,2,1,0:T(8,128)S(1)} fusion(bf16[8,10,3,128,256]{4,3,2,1,0:T(8,128)(2,1)} %bitcast.98, pred[8,10]{1,0:T(8,128)(4,1)S(1)} %copy-done.5, bf16[8,10,3,2,16,128]{5,4,3,2,1,0:T(8,128)(2,1)} %bitcast.99, pred[8,10]{1,0:T(8,128)(4,1)S(1)} %copy-done.6, bf16[8,10]{1,0:T(8,128)(2,1)S(1)} %fusion.29), kind=kOutput, calls=%fused_computation.8.clone.1 | convolution fusion | flops 513146880 | bytes 18481472 | tf_op jit(solution)/shard_map/while/body/eval_jaxpr/fsarkt,frktc->rfsac/dot_general | solution.py:75
  187.1 6.7 %collective-permute-start = (bf16[3,2,16,1024]{3,2,1,0:T(8,128)(2,1)S(1)}, bf16[3,2,16,1024]{3,2,1,0:T(8,128)(2,1)S(1)}, u32[]{:S(2)}, u32[]{:S(2)}) collective-permute-start(bf16[3,2,16,1024]{3,2,1,0:T(8,128)(2,1)S(1)} %get-tuple-element.365), channel_id=1, source_target_pairs={{2,0},{4,2},{6,4},{8,6},{10,8},{12,10},{14,12},{16,14},{18,16},{20... | collective-permute-start | bytes 589832 | tf_op jit(solution)/shard_map/while/body/eval_jaxpr/ppermute | solution.py:19
  200.1 8.2 %gather_fusion = bf16[80,3,128,256]{3,2,1,0:T(8,128)(2,1)} fusion(bf16[3,8,128,256]{3,2,1,0:T(8,128)(2,1)S(1)} %dynamic-slice_bitcast_fusion.2, s32[1024]{0:T(1024)S(1)} %pad_clamp_fusion.4), kind=kCustom, calls=%fused_computation.1.clone.1 | custom fusion | bytes 31457600 | tf_op jit(solution)/shard_map/while/body/eval_jaxpr/jit(_take)/gather | solution.py:74
  212.4 8.0 %fusion.30 = f32[8,3,2,16,256]{4,3,2,1,0:T(8,128)S(1)} fusion(bf16[8,10,3,128,256]{4,3,2,1,0:T(8,128)(2,1)} %bitcast.98, pred[8,10]{1,0:T(8,128)(4,1)S(1)} %copy-done.5, bf16[8,10,3,2,16,128]{5,4,3,2,1,0:T(8,128)(2,1)} %bitcast.99, pred[8,10]{1,0:T(8,128)(4,1)S(1)} %copy-done.6, bf16[8,10]{1,0:T(8,128)(2,1)S(1)} %fusion.29), kind=kOutput, calls=%fused_computation.8.clone.1 | convolution fusion | flops 513146880 | bytes 18481472 | tf_op jit(solution)/shard_map/while/body/eval_jaxpr/fsarkt,frktc->rfsac/dot_general | solution.py:75
  222.2 6.7 %collective-permute-start = (bf16[3,2,16,1024]{3,2,1,0:T(8,128)(2,1)S(1)}, bf16[3,2,16,1024]{3,2,1,0:T(8,128)(2,1)S(1)}, u32[]{:S(2)}, u32[]{:S(2)}) collective-permute-start(bf16[3,2,16,1024]{3,2,1,0:T(8,128)(2,1)S(1)} %get-tuple-element.365), channel_id=1, source_target_pairs={{2,0},{4,2},{6,4},{8,6},{10,8},{12,10},{14,12},{16,14},{18,16},{20... | collective-permute-start | bytes 589832 | tf_op jit(solution)/shard_map/while/body/eval_jaxpr/ppermute | solution.py:19
  235.1 8.1 %gather_fusion = bf16[80,3,128,256]{3,2,1,0:T(8,128)(2,1)} fusion(bf16[3,8,128,256]{3,2,1,0:T(8,128)(2,1)S(1)} %dynamic-slice_bitcast_fusion.2, s32[1024]{0:T(1024)S(1)} %pad_clamp_fusion.4), kind=kCustom, calls=%fused_computation.1.clone.1 | custom fusion | bytes 31457600 | tf_op jit(solution)/shard_map/while/body/eval_jaxpr/jit(_take)/gather | solution.py:74
  245.1 2.4 gather_fusion.1
  247.5 8.0 %fusion.30 = f32[8,3,2,16,256]{4,3,2,1,0:T(8,128)S(1)} fusion(bf16[8,10,3,128,256]{4,3,2,1,0:T(8,128)(2,1)} %bitcast.98, pred[8,10]{1,0:T(8,128)(4,1)S(1)} %copy-done.5, bf16[8,10,3,2,16,128]{5,4,3,2,1,0:T(8,128)(2,1)} %bitcast.99, pred[8,10]{1,0:T(8,128)(4,1)S(1)} %copy-done.6, bf16[8,10]{1,0:T(8,128)(2,1)S(1)} %fusion.29), kind=kOutput, calls=%fused_computation.8.clone.1 | convolution fusion | flops 513146880 | bytes 18481472 | tf_op jit(solution)/shard_map/while/body/eval_jaxpr/fsarkt,frktc->rfsac/dot_general | solution.py:75
  257.3 6.7 %collective-permute-start = (bf16[3,2,16,1024]{3,2,1,0:T(8,128)(2,1)S(1)}, bf16[3,2,16,1024]{3,2,1,0:T(8,128)(2,1)S(1)}, u32[]{:S(2)}, u32[]{:S(2)}) collective-permute-start(bf16[3,2,16,1024]{3,2,1,0:T(8,128)(2,1)S(1)} %get-tuple-element.365), channel_id=1, source_target_pairs={{2,0},{4,2},{6,4},{8,6},{10,8},{12,10},{14,12},{16,14},{18,16},{20... | collective-permute-start | bytes 589832 | tf_op jit(solution)/shard_map/while/body/eval_jaxpr/ppermute | solution.py:19
  270.3 8.2 %gather_fusion = bf16[80,3,128,256]{3,2,1,0:T(8,128)(2,1)} fusion(bf16[3,8,128,256]{3,2,1,0:T(8,128)(2,1)S(1)} %dynamic-slice_bitcast_fusion.2, s32[1024]{0:T(1024)S(1)} %pad_clamp_fusion.4), kind=kCustom, calls=%fused_computation.1.clone.1 | custom fusion | bytes 31457600 | tf_op jit(solution)/shard_map/while/body/eval_jaxpr/jit(_take)/gather | solution.py:74
  282.7 8.0 %fusion.30 = f32[8,3,2,16,256]{4,3,2,1,0:T(8,128)S(1)} fusion(bf16[8,10,3,128,256]{4,3,2,1,0:T(8,128)(2,1)} %bitcast.98, pred[8,10]{1,0:T(8,128)(4,1)S(1)} %copy-done.5, bf16[8,10,3,2,16,128]{5,4,3,2,1,0:T(8,128)(2,1)} %bitcast.99, pred[8,10]{1,0:T(8,128)(4,1)S(1)} %copy-done.6, bf16[8,10]{1,0:T(8,128)(2,1)S(1)} %fusion.29), kind=kOutput, calls=%fused_computation.8.clone.1 | convolution fusion | flops 513146880 | bytes 18481472 | tf_op jit(solution)/shard_map/while/body/eval_jaxpr/fsarkt,frktc->rfsac/dot_general | solution.py:75
  292.4 6.7 %collective-permute-start = (bf16[3,2,16,1024]{3,2,1,0:T(8,128)(2,1)S(1)}, bf16[3,2,16,1024]{3,2,1,0:T(8,128)(2,1)S(1)}, u32[]{:S(2)}, u32[]{:S(2)}) collective-permute-start(bf16[3,2,16,1024]{3,2,1,0:T(8,128)(2,1)S(1)} %get-tuple-element.365), channel_id=1, source_target_pairs={{2,0},{4,2},{6,4},{8,6},{10,8},{12,10},{14,12},{16,14},{18,16},{20... | collective-permute-start | bytes 589832 | tf_op jit(solution)/shard_map/while/body/eval_jaxpr/ppermute | solution.py:19
  305.4 8.1 %gather_fusion = bf16[80,3,128,256]{3,2,1,0:T(8,128)(2,1)} fusion(bf16[3,8,128,256]{3,2,1,0:T(8,128)(2,1)S(1)} %dynamic-slice_bitcast_fusion.2, s32[1024]{0:T(1024)S(1)} %pad_clamp_fusion.4), kind=kCustom, calls=%fused_computation.1.clone.1 | custom fusion | bytes 31457600 | tf_op jit(solution)/shard_map/while/body/eval_jaxpr/jit(_take)/gather | solution.py:74
  315.3 2.4 gather_fusion.1
  317.7 8.0 %fusion.30 = f32[8,3,2,16,256]{4,3,2,1,0:T(8,128)S(1)} fusion(bf16[8,10,3,128,256]{4,3,2,1,0:T(8,128)(2,1)} %bitcast.98, pred[8,10]{1,0:T(8,128)(4,1)S(1)} %copy-done.5, bf16[8,10,3,2,16,128]{5,4,3,2,1,0:T(8,128)(2,1)} %bitcast.99, pred[8,10]{1,0:T(8,128)(4,1)S(1)} %copy-done.6, bf16[8,10]{1,0:T(8,128)(2,1)S(1)} %fusion.29), kind=kOutput, calls=%fused_computation.8.clone.1 | convolution fusion | flops 513146880 | bytes 18481472 | tf_op jit(solution)/shard_map/while/body/eval_jaxpr/fsarkt,frktc->rfsac/dot_general | solution.py:75
  327.5 6.7 %collective-permute-start = (bf16[3,2,16,1024]{3,2,1,0:T(8,128)(2,1)S(1)}, bf16[3,2,16,1024]{3,2,1,0:T(8,128)(2,1)S(1)}, u32[]{:S(2)}, u32[]{:S(2)}) collective-permute-start(bf16[3,2,16,1024]{3,2,1,0:T(8,128)(2,1)S(1)} %get-tuple-element.365), channel_id=1, source_target_pairs={{2,0},{4,2},{6,4},{8,6},{10,8},{12,10},{14,12},{16,14},{18,16},{20... | collective-permute-start | bytes 589832 | tf_op jit(solution)/shard_map/while/body/eval_jaxpr/ppermute | solution.py:19
  340.5 8.2 %gather_fusion = bf16[80,3,128,256]{3,2,1,0:T(8,128)(2,1)} fusion(bf16[3,8,128,256]{3,2,1,0:T(8,128)(2,1)S(1)} %dynamic-slice_bitcast_fusion.2, s32[1024]{0:T(1024)S(1)} %pad_clamp_fusion.4), kind=kCustom, calls=%fused_computation.1.clone.1 | custom fusion | bytes 31457600 | tf_op jit(solution)/shard_map/while/body/eval_jaxpr/jit(_take)/gather | solution.py:74
  352.9 8.0 %fusion.30 = f32[8,3,2,16,256]{4,3,2,1,0:T(8,128)S(1)} fusion(bf16[8,10,3,128,256]{4,3,2,1,0:T(8,128)(2,1)} %bitcast.98, pred[8,10]{1,0:T(8,128)(4,1)S(1)} %copy-done.5, bf16[8,10,3,2,16,128]{5,4,3,2,1,0:T(8,128)(2,1)} %bitcast.99, pred[8,10]{1,0:T(8,128)(4,1)S(1)} %copy-done.6, bf16[8,10]{1,0:T(8,128)(2,1)S(1)} %fusion.29), kind=kOutput, calls=%fused_computation.8.clone.1 | convolution fusion | flops 513146880 | bytes 18481472 | tf_op jit(solution)/shard_map/while/body/eval_jaxpr/fsarkt,frktc->rfsac/dot_general | solution.py:75
  362.7 6.6 %collective-permute-start = (bf16[3,2,16,1024]{3,2,1,0:T(8,128)(2,1)S(1)}, bf16[3,2,16,1024]{3,2,1,0:T(8,128)(2,1)S(1)}, u32[]{:S(2)}, u32[]{:S(2)}) collective-permute-start(bf16[3,2,16,1024]{3,2,1,0:T(8,128)(2,1)S(1)} %get-tuple-element.365), channel_id=1, source_target_pairs={{2,0},{4,2},{6,4},{8,6},{10,8},{12,10},{14,12},{16,14},{18,16},{20... | collective-permute-start | bytes 589832 | tf_op jit(solution)/shard_map/while/body/eval_jaxpr/ppermute | solution.py:19
  375.6 8.2 %gather_fusion = bf16[80,3,128,256]{3,2,1,0:T(8,128)(2,1)} fusion(bf16[3,8,128,256]{3,2,1,0:T(8,128)(2,1)S(1)} %dynamic-slice_bitcast_fusion.2, s32[1024]{0:T(1024)S(1)} %pad_clamp_fusion.4), kind=kCustom, calls=%fused_computation.1.clone.1 | custom fusion | bytes 31457600 | tf_op jit(solution)/shard_map/while/body/eval_jaxpr/jit(_take)/gather | solution.py:74
  387.9 8.0 %fusion.30 = f32[8,3,2,16,256]{4,3,2,1,0:T(8,128)S(1)} fusion(bf16[8,10,3,128,256]{4,3,2,1,0:T(8,128)(2,1)} %bitcast.98, pred[8,10]{1,0:T(8,128)(4,1)S(1)} %copy-done.5, bf16[8,10,3,2,16,128]{5,4,3,2,1,0:T(8,128)(2,1)} %bitcast.99, pred[8,10]{1,0:T(8,128)(4,1)S(1)} %copy-done.6, bf16[8,10]{1,0:T(8,128)(2,1)S(1)} %fusion.29), kind=kOutput, calls=%fused_computation.8.clone.1 | convolution fusion | flops 513146880 | bytes 18481472 | tf_op jit(solution)/shard_map/while/body/eval_jaxpr/fsarkt,frktc->rfsac/dot_general | solution.py:75
  397.7 6.7 %collective-permute-start = (bf16[3,2,16,1024]{3,2,1,0:T(8,128)(2,1)S(1)}, bf16[3,2,16,1024]{3,2,1,0:T(8,128)(2,1)S(1)}, u32[]{:S(2)}, u32[]{:S(2)}) collective-permute-start(bf16[3,2,16,1024]{3,2,1,0:T(8,128)(2,1)S(1)} %get-tuple-element.365), channel_id=1, source_target_pairs={{2,0},{4,2},{6,4},{8,6},{10,8},{12,10},{14,12},{16,14},{18,16},{20... | collective-permute-start | bytes 589832 | tf_op jit(solution)/shard_map/while/body/eval_jaxpr/ppermute | solution.py:19
  410.7 8.2 %gather_fusion = bf16[80,3,128,256]{3,2,1,0:T(8,128)(2,1)} fusion(bf16[3,8,128,256]{3,2,1,0:T(8,128)(2,1)S(1)} %dynamic-slice_bitcast_fusion.2, s32[1024]{0:T(1024)S(1)} %pad_clamp_fusion.4), kind=kCustom, calls=%fused_computation.1.clone.1 | custom fusion | bytes 31457600 | tf_op jit(solution)/shard_map/while/body/eval_jaxpr/jit(_take)/gather | solution.py:74
  423.0 8.0 %fusion.30 = f32[8,3,2,16,256]{4,3,2,1,0:T(8,128)S(1)} fusion(bf16[8,10,3,128,256]{4,3,2,1,0:T(8,128)(2,1)} %bitcast.98, pred[8,10]{1,0:T(8,128)(4,1)S(1)} %copy-done.5, bf16[8,10,3,2,16,128]{5,4,3,2,1,0:T(8,128)(2,1)} %bitcast.99, pred[8,10]{1,0:T(8,128)(4,1)S(1)} %copy-done.6, bf16[8,10]{1,0:T(8,128)(2,1)S(1)} %fusion.29), kind=kOutput, calls=%fused_computation.8.clone.1 | convolution fusion | flops 513146880 | bytes 18481472 | tf_op jit(solution)/shard_map/while/body/eval_jaxpr/fsarkt,frktc->rfsac/dot_general | solution.py:75
  433.6 10.9 %all_to_all.10 = f32[8,1,1024]{2,1,0:T(1,128)S(1)} all-to-all(f32[8,1,1024]{2,1,0:T(1,128)S(1)} %reshape.218), channel_id=1, replica_groups=mesh['depth'=8,'lat'=32,'freq'=2] {'depth'}, dimensions={0} | all-to-all | bytes 65536 | tf_op jit(solution)/shard_map/all_to_all | solution.py:58
  444.5 8.4 %psum.7 = f32[1024]{0:T(1024)S(1)} all-reduce(f32[1024]{0:T(1024)S(1)} %reduce_sum.20), channel_id=1, replica_groups=mesh['depth'=8,'lat'=32,'freq'=2] {'freq'}, use_global_device_ids=true, to_apply=%region_4.5 | all-reduce | flops 1024 | bytes 8192 | tf_op jit(solution)/shard_map/psum | solution.py:119
  (263 shorter events, 98.5 us)
Async XLA Ops:
  6.5 32.0 %copy-start = (bf16[3,2,128,1024]{3,2,1,0:T(8,128)(2,1)S(1)}, bf16[3,2,128,1024]{3,2,1,0:T(8,128)(2,1)}, u32[]{:S(2)}) copy-start(bf16[3,2,128,1024]{3,2,1,0:T(8,128)(2,1)} %param.8) | copy-start | bytes 4718596
  6.5 144.3 %all-gather.2.cloned.1.call-start = ((), (), s32[]{:S(2)}) async-start(), calls=%async_computation.2 | async-start | bytes 14155776 | tf_op jit(solution)/shard_map/all_gather | solution.py:97
  8.6 30.8 %all-to-all-start = ((f32[8,1,1024]{2,1,0:T(1,128)}), f32[8,1,1024]{2,1,0:T(1,128)S(1)}, u32[]{:S(2)}, u32[]{:S(2)}) async-start(f32[8,1,1024]{2,1,0:T(1,128)} %broadcast_in_dim.88), calls=%async_computation | async-start | bytes 65536 | tf_op jit(solution)/shard_map/all_to_all | solution.py:37
  150.9 10.4 %copy-start.1 = (s32[8,8,10]{2,1,0:T(8,128)}, s32[8,8,10]{2,1,0:T(8,128)S(1)}, u32[]{:S(2)}) copy-start(s32[8,8,10]{2,1,0:T(8,128)S(1)} %get-tuple-element.381) | copy-start | bytes 7684 | tf_op jit(solution)/shard_map/while
  150.9 10.4 %copy-start.3 = (s32[8,8,10]{2,1,0:T(8,128)}, s32[8,8,10]{2,1,0:T(8,128)S(1)}, u32[]{:S(2)}) copy-start(s32[8,8,10]{2,1,0:T(8,128)S(1)} %get-tuple-element.378) | copy-start | bytes 7684 | tf_op jit(solution)/shard_map/while
  150.9 22.9 %collective-permute-start = (bf16[3,2,16,1024]{3,2,1,0:T(8,128)(2,1)S(1)}, bf16[3,2,16,1024]{3,2,1,0:T(8,128)(2,1)S(1)}, u32[]{:S(2)}, u32[]{:S(2)}) collective-permute-start(bf16[3,2,16,1024]{3,2,1,0:T(8,128)(2,1)S(1)} %get-tuple-element.365), channel_id=1, source_target_pairs={{2,0},{4,2},{6,4},{8,6},{10,8},{12,10},{14,12},{16,14},{18,16},{20... | collective-permute-start | bytes 589832 | tf_op jit(solution)/shard_map/while/body/eval_jaxpr/ppermute | solution.py:19
  158.7 15.1 %collective-permute-start.1 = (bf16[3,2,16,1024]{3,2,1,0:T(8,128)(2,1)S(1)}, bf16[3,2,16,1024]{3,2,1,0:T(8,128)(2,1)}, u32[]{:S(2)}, u32[]{:S(2)}) collective-permute-start(bf16[3,2,16,1024]{3,2,1,0:T(8,128)(2,1)S(1)} %get-tuple-element.365), channel_id=1, source_target_pairs={{0,2},{2,4},{4,6},{6,8},{8,10},{10,12},{12,14},{14,16},{16,18},{18... | collective-permute-start | bytes 589832 | tf_op jit(solution)/shard_map/while/body/eval_jaxpr/ppermute | solution.py:16
  187.0 9.4 %copy-start.1 = (s32[8,8,10]{2,1,0:T(8,128)}, s32[8,8,10]{2,1,0:T(8,128)S(1)}, u32[]{:S(2)}) copy-start(s32[8,8,10]{2,1,0:T(8,128)S(1)} %get-tuple-element.381) | copy-start | bytes 7684 | tf_op jit(solution)/shard_map/while
  187.0 9.4 %copy-start.3 = (s32[8,8,10]{2,1,0:T(8,128)}, s32[8,8,10]{2,1,0:T(8,128)S(1)}, u32[]{:S(2)}) copy-start(s32[8,8,10]{2,1,0:T(8,128)S(1)} %get-tuple-element.378) | copy-start | bytes 7684 | tf_op jit(solution)/shard_map/while
  187.1 21.9 %collective-permute-start = (bf16[3,2,16,1024]{3,2,1,0:T(8,128)(2,1)S(1)}, bf16[3,2,16,1024]{3,2,1,0:T(8,128)(2,1)S(1)}, u32[]{:S(2)}, u32[]{:S(2)}) collective-permute-start(bf16[3,2,16,1024]{3,2,1,0:T(8,128)(2,1)S(1)} %get-tuple-element.365), channel_id=1, source_target_pairs={{2,0},{4,2},{6,4},{8,6},{10,8},{12,10},{14,12},{16,14},{18,16},{20... | collective-permute-start | bytes 589832 | tf_op jit(solution)/shard_map/while/body/eval_jaxpr/ppermute | solution.py:19
  193.8 15.2 %collective-permute-start.1 = (bf16[3,2,16,1024]{3,2,1,0:T(8,128)(2,1)S(1)}, bf16[3,2,16,1024]{3,2,1,0:T(8,128)(2,1)}, u32[]{:S(2)}, u32[]{:S(2)}) collective-permute-start(bf16[3,2,16,1024]{3,2,1,0:T(8,128)(2,1)S(1)} %get-tuple-element.365), channel_id=1, source_target_pairs={{0,2},{2,4},{4,6},{6,8},{8,10},{10,12},{12,14},{14,16},{16,18},{18... | collective-permute-start | bytes 589832 | tf_op jit(solution)/shard_map/while/body/eval_jaxpr/ppermute | solution.py:16
  222.2 9.3 %copy-start.1 = (s32[8,8,10]{2,1,0:T(8,128)}, s32[8,8,10]{2,1,0:T(8,128)S(1)}, u32[]{:S(2)}) copy-start(s32[8,8,10]{2,1,0:T(8,128)S(1)} %get-tuple-element.381) | copy-start | bytes 7684 | tf_op jit(solution)/shard_map/while
  222.2 9.3 %copy-start.3 = (s32[8,8,10]{2,1,0:T(8,128)}, s32[8,8,10]{2,1,0:T(8,128)S(1)}, u32[]{:S(2)}) copy-start(s32[8,8,10]{2,1,0:T(8,128)S(1)} %get-tuple-element.378) | copy-start | bytes 7684 | tf_op jit(solution)/shard_map/while
  222.2 21.8 %collective-permute-start = (bf16[3,2,16,1024]{3,2,1,0:T(8,128)(2,1)S(1)}, bf16[3,2,16,1024]{3,2,1,0:T(8,128)(2,1)S(1)}, u32[]{:S(2)}, u32[]{:S(2)}) collective-permute-start(bf16[3,2,16,1024]{3,2,1,0:T(8,128)(2,1)S(1)} %get-tuple-element.365), channel_id=1, source_target_pairs={{2,0},{4,2},{6,4},{8,6},{10,8},{12,10},{14,12},{16,14},{18,16},{20... | collective-permute-start | bytes 589832 | tf_op jit(solution)/shard_map/while/body/eval_jaxpr/ppermute | solution.py:19
  228.9 15.1 %collective-permute-start.1 = (bf16[3,2,16,1024]{3,2,1,0:T(8,128)(2,1)S(1)}, bf16[3,2,16,1024]{3,2,1,0:T(8,128)(2,1)}, u32[]{:S(2)}, u32[]{:S(2)}) collective-permute-start(bf16[3,2,16,1024]{3,2,1,0:T(8,128)(2,1)S(1)} %get-tuple-element.365), channel_id=1, source_target_pairs={{0,2},{2,4},{4,6},{6,8},{8,10},{10,12},{12,14},{14,16},{16,18},{18... | collective-permute-start | bytes 589832 | tf_op jit(solution)/shard_map/while/body/eval_jaxpr/ppermute | solution.py:16
  257.3 9.4 %copy-start.1 = (s32[8,8,10]{2,1,0:T(8,128)}, s32[8,8,10]{2,1,0:T(8,128)S(1)}, u32[]{:S(2)}) copy-start(s32[8,8,10]{2,1,0:T(8,128)S(1)} %get-tuple-element.381) | copy-start | bytes 7684 | tf_op jit(solution)/shard_map/while
  257.3 9.4 %copy-start.3 = (s32[8,8,10]{2,1,0:T(8,128)}, s32[8,8,10]{2,1,0:T(8,128)S(1)}, u32[]{:S(2)}) copy-start(s32[8,8,10]{2,1,0:T(8,128)S(1)} %get-tuple-element.378) | copy-start | bytes 7684 | tf_op jit(solution)/shard_map/while
  257.3 21.9 %collective-permute-start = (bf16[3,2,16,1024]{3,2,1,0:T(8,128)(2,1)S(1)}, bf16[3,2,16,1024]{3,2,1,0:T(8,128)(2,1)S(1)}, u32[]{:S(2)}, u32[]{:S(2)}) collective-permute-start(bf16[3,2,16,1024]{3,2,1,0:T(8,128)(2,1)S(1)} %get-tuple-element.365), channel_id=1, source_target_pairs={{2,0},{4,2},{6,4},{8,6},{10,8},{12,10},{14,12},{16,14},{18,16},{20... | collective-permute-start | bytes 589832 | tf_op jit(solution)/shard_map/while/body/eval_jaxpr/ppermute | solution.py:19
  264.0 15.2 %collective-permute-start.1 = (bf16[3,2,16,1024]{3,2,1,0:T(8,128)(2,1)S(1)}, bf16[3,2,16,1024]{3,2,1,0:T(8,128)(2,1)}, u32[]{:S(2)}, u32[]{:S(2)}) collective-permute-start(bf16[3,2,16,1024]{3,2,1,0:T(8,128)(2,1)S(1)} %get-tuple-element.365), channel_id=1, source_target_pairs={{0,2},{2,4},{4,6},{6,8},{8,10},{10,12},{12,14},{14,16},{16,18},{18... | collective-permute-start | bytes 589832 | tf_op jit(solution)/shard_map/while/body/eval_jaxpr/ppermute | solution.py:16
  292.4 9.3 %copy-start.3 = (s32[8,8,10]{2,1,0:T(8,128)}, s32[8,8,10]{2,1,0:T(8,128)S(1)}, u32[]{:S(2)}) copy-start(s32[8,8,10]{2,1,0:T(8,128)S(1)} %get-tuple-element.378) | copy-start | bytes 7684 | tf_op jit(solution)/shard_map/while
  292.4 21.8 %collective-permute-start = (bf16[3,2,16,1024]{3,2,1,0:T(8,128)(2,1)S(1)}, bf16[3,2,16,1024]{3,2,1,0:T(8,128)(2,1)S(1)}, u32[]{:S(2)}, u32[]{:S(2)}) collective-permute-start(bf16[3,2,16,1024]{3,2,1,0:T(8,128)(2,1)S(1)} %get-tuple-element.365), channel_id=1, source_target_pairs={{2,0},{4,2},{6,4},{8,6},{10,8},{12,10},{14,12},{16,14},{18,16},{20... | collective-permute-start | bytes 589832 | tf_op jit(solution)/shard_map/while/body/eval_jaxpr/ppermute | solution.py:19
  299.1 15.1 %collective-permute-start.1 = (bf16[3,2,16,1024]{3,2,1,0:T(8,128)(2,1)S(1)}, bf16[3,2,16,1024]{3,2,1,0:T(8,128)(2,1)}, u32[]{:S(2)}, u32[]{:S(2)}) collective-permute-start(bf16[3,2,16,1024]{3,2,1,0:T(8,128)(2,1)S(1)} %get-tuple-element.365), channel_id=1, source_target_pairs={{0,2},{2,4},{4,6},{6,8},{8,10},{10,12},{12,14},{14,16},{16,18},{18... | collective-permute-start | bytes 589832 | tf_op jit(solution)/shard_map/while/body/eval_jaxpr/ppermute | solution.py:16
  327.5 9.4 %copy-start.1 = (s32[8,8,10]{2,1,0:T(8,128)}, s32[8,8,10]{2,1,0:T(8,128)S(1)}, u32[]{:S(2)}) copy-start(s32[8,8,10]{2,1,0:T(8,128)S(1)} %get-tuple-element.381) | copy-start | bytes 7684 | tf_op jit(solution)/shard_map/while
  327.5 9.4 %copy-start.3 = (s32[8,8,10]{2,1,0:T(8,128)}, s32[8,8,10]{2,1,0:T(8,128)S(1)}, u32[]{:S(2)}) copy-start(s32[8,8,10]{2,1,0:T(8,128)S(1)} %get-tuple-element.378) | copy-start | bytes 7684 | tf_op jit(solution)/shard_map/while
  327.5 21.9 %collective-permute-start = (bf16[3,2,16,1024]{3,2,1,0:T(8,128)(2,1)S(1)}, bf16[3,2,16,1024]{3,2,1,0:T(8,128)(2,1)S(1)}, u32[]{:S(2)}, u32[]{:S(2)}) collective-permute-start(bf16[3,2,16,1024]{3,2,1,0:T(8,128)(2,1)S(1)} %get-tuple-element.365), channel_id=1, source_target_pairs={{2,0},{4,2},{6,4},{8,6},{10,8},{12,10},{14,12},{16,14},{18,16},{20... | collective-permute-start | bytes 589832 | tf_op jit(solution)/shard_map/while/body/eval_jaxpr/ppermute | solution.py:19
  334.2 15.2 %collective-permute-start.1 = (bf16[3,2,16,1024]{3,2,1,0:T(8,128)(2,1)S(1)}, bf16[3,2,16,1024]{3,2,1,0:T(8,128)(2,1)}, u32[]{:S(2)}, u32[]{:S(2)}) collective-permute-start(bf16[3,2,16,1024]{3,2,1,0:T(8,128)(2,1)S(1)} %get-tuple-element.365), channel_id=1, source_target_pairs={{0,2},{2,4},{4,6},{6,8},{8,10},{10,12},{12,14},{14,16},{16,18},{18... | collective-permute-start | bytes 589832 | tf_op jit(solution)/shard_map/while/body/eval_jaxpr/ppermute | solution.py:16
  362.7 21.8 %collective-permute-start = (bf16[3,2,16,1024]{3,2,1,0:T(8,128)(2,1)S(1)}, bf16[3,2,16,1024]{3,2,1,0:T(8,128)(2,1)S(1)}, u32[]{:S(2)}, u32[]{:S(2)}) collective-permute-start(bf16[3,2,16,1024]{3,2,1,0:T(8,128)(2,1)S(1)} %get-tuple-element.365), channel_id=1, source_target_pairs={{2,0},{4,2},{6,4},{8,6},{10,8},{12,10},{14,12},{16,14},{18,16},{20... | collective-permute-start | bytes 589832 | tf_op jit(solution)/shard_map/while/body/eval_jaxpr/ppermute | solution.py:19
  369.3 15.2 %collective-permute-start.1 = (bf16[3,2,16,1024]{3,2,1,0:T(8,128)(2,1)S(1)}, bf16[3,2,16,1024]{3,2,1,0:T(8,128)(2,1)}, u32[]{:S(2)}, u32[]{:S(2)}) collective-permute-start(bf16[3,2,16,1024]{3,2,1,0:T(8,128)(2,1)S(1)} %get-tuple-element.365), channel_id=1, source_target_pairs={{0,2},{2,4},{4,6},{6,8},{8,10},{10,12},{12,14},{14,16},{16,18},{18... | collective-permute-start | bytes 589832 | tf_op jit(solution)/shard_map/while/body/eval_jaxpr/ppermute | solution.py:16
  397.7 9.3 %copy-start.1 = (s32[8,8,10]{2,1,0:T(8,128)}, s32[8,8,10]{2,1,0:T(8,128)S(1)}, u32[]{:S(2)}) copy-start(s32[8,8,10]{2,1,0:T(8,128)S(1)} %get-tuple-element.381) | copy-start | bytes 7684 | tf_op jit(solution)/shard_map/while
  397.7 9.4 %copy-start.3 = (s32[8,8,10]{2,1,0:T(8,128)}, s32[8,8,10]{2,1,0:T(8,128)S(1)}, u32[]{:S(2)}) copy-start(s32[8,8,10]{2,1,0:T(8,128)S(1)} %get-tuple-element.378) | copy-start | bytes 7684 | tf_op jit(solution)/shard_map/while
  397.7 21.8 %collective-permute-start = (bf16[3,2,16,1024]{3,2,1,0:T(8,128)(2,1)S(1)}, bf16[3,2,16,1024]{3,2,1,0:T(8,128)(2,1)S(1)}, u32[]{:S(2)}, u32[]{:S(2)}) collective-permute-start(bf16[3,2,16,1024]{3,2,1,0:T(8,128)(2,1)S(1)} %get-tuple-element.365), channel_id=1, source_target_pairs={{2,0},{4,2},{6,4},{8,6},{10,8},{12,10},{14,12},{16,14},{18,16},{20... | collective-permute-start | bytes 589832 | tf_op jit(solution)/shard_map/while/body/eval_jaxpr/ppermute | solution.py:19
  404.4 15.1 %collective-permute-start.1 = (bf16[3,2,16,1024]{3,2,1,0:T(8,128)(2,1)S(1)}, bf16[3,2,16,1024]{3,2,1,0:T(8,128)(2,1)}, u32[]{:S(2)}, u32[]{:S(2)}) collective-permute-start(bf16[3,2,16,1024]{3,2,1,0:T(8,128)(2,1)S(1)} %get-tuple-element.365), channel_id=1, source_target_pairs={{0,2},{2,4},{4,6},{6,8},{8,10},{10,12},{12,14},{14,16},{16,18},{18... | collective-permute-start | bytes 589832 | tf_op jit(solution)/shard_map/while/body/eval_jaxpr/ppermute | solution.py:16
  (35 other events, 94.3 us)
Sparse Core Ops, SparseCore 0:
  9.4 141.3 all-gather.1
where the time goes:
time: 463 us; the launch traced here: 460 us
  local copies, waits for them, and re-layouts  114 us (25%)
  waiting for transfers between devices  112 us (24%)
  starting transfers between devices  77.6 us (17%)
  matrix products  64.4 us (14%)
  blocking collectives  40.1 us (9%)
  other arithmetic  38.8 us (8%)
  between operations  13.4 us (3%)
    all_gather x1, waiting for transfers between devices, per_device(): pool_all = lax.all_gather(pool, 'depth', axis=0, tiled=True)  111 us
    gather x8, local copies, waits for them, and re-layouts, extrapolate(): chosen = jnp.take(pool_level, block_level, axis=1)  65.3 us
    dot_general x8, matrix products, extrapolate(): jnp.einsum('fsarkt,frktc->rfsac', picked, chosen, preferred_element_type=...  64.4 us
    ppermute x8, starting transfers between devices, extended_2(): lax.ppermute(lax.slice_in_dim(block, 0, width, axis=dim), axis, backward)  54.6 us
    all_gather x1, blocking collectives, in_one_piece(): lax.all_gather(both, axis, axis=dim, tiled=True)  20.8 us
    gather x8, local copies, waits for them, and re-layouts, extrapolate(): jnp.take(tile_grid, local_ids, axis=3)  19.3 us
    ppermute x8, starting transfers between devices, extended_2(): lax.ppermute(lax.slice_in_dim(block, block.shape[dim] - width, None, axis...  15.4 us
    squeeze x8, local copies, waits for them, and re-layouts, level_step(): lax.dynamic_index_in_dim(pool_all, level_index, 0, keepdims=False)  12.1 us
  transfers between devices with their start and end apart: 18, of which 1 were waited for; matrix products, arithmetic and copies ran while one was open for 24% of the time, Pallas kernels for 0%

commit v1 on v0

--- a/solution.py
+++ b/solution.py
@@ -94,7 +94,24 @@
     lateral_width = surface.shape[3]
     shot_rows = shot_total // lax.axis_size("depth")
     own_shots = lax.dynamic_slice_in_dim(surface, depth_index * shot_rows, shot_rows, 2)
-    pool_all = lax.all_gather(pool, "depth", axis=0, tiled=True)
+    devices, mine, rows = (lax.axis_size("depth"), lax.axis_index("depth"), pool.shape[0])
+    forward_2 = [(i_2, (i_2 + 1) % devices) for i_2 in range(devices)]
+    downward = [(i_2, (i_2 - 1) % devices) for i_2 in range(devices)]
+    filled = jnp.zeros((*pool.shape[:0], devices * rows, *pool.shape[0 + 1 :]), pool.dtype)
+    filled = lax.dynamic_update_slice_in_dim(filled, pool, mine * rows, axis=0)
+    from_left = from_right = pool
+    half = devices // 2
+    for lap in range(1, half + 1):
+        from_left = lax.ppermute(from_left, "depth", forward_2)
+        filled = lax.dynamic_update_slice_in_dim(
+            filled, from_left, (mine - lap) % devices * rows, axis=0
+        )
+        if lap < devices - half:
+            from_right = lax.ppermute(from_right, "depth", downward)
+            filled = lax.dynamic_update_slice_in_dim(
+                filled, from_right, (mine + lap) % devices * rows, axis=0
+            )
+    pool_all = filled
     ids_all, blocks_all, counts_all = in_one_piece((tile_ids, block_ids, counts), "depth", 0, 2)
     refl_all = gather_directly(refl, "depth", 0)
     level_total = pool_all.shape[0]

time: 463 us -> 521 us (1.13)
  starting transfers between devices: 77.6 us -> 112 us
  blocking collectives: 40.1 us -> 69.1 us
  waiting for transfers between devices: 112 us -> 86.3 us
  local copies, waits for them, and re-layouts: 114 us -> 136 us
  between operations: 13.4 us -> 0.22 us
  other arithmetic: 38.8 us -> 49.2 us
    all_gather x1 -> x0, waiting for transfers between devices: 111 us -> none  [per_device(): pool_all = lax.all_gather(pool, 'depth', axis=0, tiled=True)]
    ppermute x0 -> x7, waiting for transfers between devices: none -> 86.2 us  [the longest x4 85.9 us: per_device(): from_left = lax.ppermute(from_left, 'depth', forward_2)]
    ppermute x0 -> x7, starting transfers between devices: none -> 26.6 us  [the longest x4 14.4 us: per_device(): from_left = lax.ppermute(from_left, 'depth', forward_2)]
    all_gather x1, blocking collectives: 20.8 us -> 40.1 us  [in_one_piece(): lax.all_gather(both, axis, axis=dim, tiled=True)]
    dynamic_update_slice x0 -> x8, local copies, waits for them, and re-layouts: none -> 16 us  [the longest x4 8.04 us: per_device(): lax.dynamic_update_slice_in_dim(filled, from_left, (mine - lap) % devices...]
    psum x1, blocking collectives: 8.41 us -> 17.5 us  [per_device(): summed = lax.psum(image_local, 'freq')]
    broadcast_in_dim x0 -> x1, local copies, waits for them, and re-layouts: none -> 6.24 us  [per_device(): jnp.zeros((*pool.shape[:0], devices * rows, *pool.shape[0 + 1:]), pool.dt...]
    and x8, other arithmetic: 4.85 us -> 10.4 us  [extrapolate(): chosen = jnp.take(pool_level, block_level, axis=1)]
  transfers between devices with their start and end apart: 18 -> 24, of which waited for: 1 -> 4; matrix products, arithmetic and copies ran while one was open for 24% -> 27% of each run, Pallas kernels for 0% -> 0%
where the time goes in v1:
time: 521 us; the launch traced here: 518 us
  local copies, waits for them, and re-layouts  136 us (26%)
  starting transfers between devices  112 us (21%)
  waiting for transfers between devices  86.3 us (17%)
  blocking collectives  69.1 us (13%)
  matrix products  64.4 us (12%)
  other arithmetic  49.2 us (9%)
    ppermute x4, waiting for transfers between devices, per_device(): from_left = lax.ppermute(from_left, 'depth', forward_2)  85.9 us
    gather x8, local copies, waits for them, and re-layouts, extrapolate(): chosen = jnp.take(pool_level, block_level, axis=1)  65.2 us
    dot_general x8, matrix products, extrapolate(): jnp.einsum('fsarkt,frktc->rfsac', picked, chosen, preferred_element_type=...  64.4 us
    ppermute x8, starting transfers between devices, extended_2(): lax.ppermute(lax.slice_in_dim(block, 0, width, axis=dim), axis, backward)  59.9 us
    all_gather x1, blocking collectives, in_one_piece(): lax.all_gather(both, axis, axis=dim, tiled=True)  40.1 us
    gather x8, local copies, waits for them, and re-layouts, extrapolate(): jnp.take(tile_grid, local_ids, axis=3)  19.3 us
    psum x1, blocking collectives, per_device(): summed = lax.psum(image_local, 'freq')  17.5 us
    ppermute x8, starting transfers between devices, extended_2(): lax.ppermute(lax.slice_in_dim(block, block.shape[dim] - width, None, axis...  15.4 us
  transfers between devices with their start and end apart: 24, of which 4 were waited for; matrix products, arithmetic and copies ran while one was open for 27% of the time, Pallas kernels for 0%

profile of v1, /device:TPU:1, one launch (start us, length us, event | category | flops | bytes accessed | tf_op | source)
XLA Modules:
  0.0 517.6 jit_solution(12659916028505848471)
XLA Ops:
  8.0 27.2 %collective-permute-done.2 = bf16[1,3,8,128,256]{4,3,2,1,0:T(8,128)(2,1)S(1)} collective-permute-done((bf16[1,3,8,128,256]{4,3,2,1,0:T(8,128)(2,1)}, bf16[1,3,8,128,256]{4,3,2,1,0:T(8,128)(2,1)S(1)}, u32[]{:S(2)}, u32[]{:S(2)}) %collective-permute-start.2) | collective-permute-done | bytes 1572896 | tf_op jit(solution)/shard_map/ppermute | solution.py:105
  45.4 29.7 %collective-permute-done.4 = bf16[1,3,8,128,256]{4,3,2,1,0:T(8,128)(2,1)S(1)} collective-permute-done((bf16[1,3,8,128,256]{4,3,2,1,0:T(8,128)(2,1)S(1)}, bf16[1,3,8,128,256]{4,3,2,1,0:T(8,128)(2,1)S(1)}, u32[]{:S(2)}, u32[]{:S(2)}) %collective-permute-start.4) | collective-permute-done | bytes 1572896 | tf_op jit(solution)/shard_map/ppermute | solution.py:105
  81.7 29.0 %collective-permute-done.6 = bf16[1,3,8,128,256]{4,3,2,1,0:T(8,128)(2,1)} collective-permute-done((bf16[1,3,8,128,256]{4,3,2,1,0:T(8,128)(2,1)S(1)}, bf16[1,3,8,128,256]{4,3,2,1,0:T(8,128)(2,1)}, u32[]{:S(2)}, u32[]{:S(2)}) %collective-permute-start.6) | collective-permute-done | bytes 1572896 | tf_op jit(solution)/shard_map/ppermute | solution.py:105
  114.2 9.7 %all-to-all-start = ((f32[8,1,1024]{2,1,0:T(1,128)}), f32[8,1,1024]{2,1,0:T(1,128)S(1)}, u32[]{:S(2)}, u32[]{:S(2)}) async-start(f32[8,1,1024]{2,1,0:T(1,128)} %broadcast_in_dim.92), calls=%async_computation | async-start | bytes 65536 | tf_op jit(solution)/shard_map/all_to_all | solution.py:37
  125.4 40.1 %all_gather.3 = s32[8,8,21]{2,1,0:T(8,128)S(1)} all-gather(s32[1,8,21]{2,1,0:T(8,128)S(1)} %pad_add_fusion), channel_id=1, replica_groups=mesh['depth'=8,'lat'=32,'freq'=2] {'depth'}, dimensions={0}, use_global_device_ids=true | all-gather | bytes 6048 | tf_op jit(solution)/shard_map/all_gather | solution.py:27
  190.1 297.1 %while.17 = (s32[]{:T(128)}, bf16[3,2,16,1024]{3,2,1,0:T(8,128)(2,1)S(1)}, f32[8,1024]{1,0:T(8,128)}, s32[8,8,10]{2,1,0:T(8,128)}, s32[]{:T(128)}, /*index=5*/s3...) while((s32[]{:T(128)}, ...), condition=%wide.region_2.3_spmd, body=%wide.region_0.2_spmd.sunk | while | flops 515904960 | bytes 61974620 | solution.py:134
  190.1 13.2 %collective-permute-start = (bf16[3,2,16,1024]{3,2,1,0:T(8,128)(2,1)S(1)}, bf16[3,2,16,1024]{3,2,1,0:T(8,128)(2,1)S(1)}, u32[]{:S(2)}, u32[]{:S(2)}) collective-permute-start(bf16[3,2,16,1024]{3,2,1,0:T(8,128)(2,1)S(1)} %get-tuple-element.365), channel_id=1, source_target_pairs={{2,0},{4,2},{6,4},{8,6},{10,8},{12,10},{14,12},{16,14},{18,16},{20... | collective-permute-start | bytes 589832 | tf_op jit(solution)/shard_map/while/body/eval_jaxpr/ppermute | solution.py:19
  210.8 8.1 %gather_fusion = bf16[80,3,128,256]{3,2,1,0:T(8,128)(2,1)} fusion(bf16[3,8,128,256]{3,2,1,0:T(8,128)(2,1)S(1)} %dynamic-slice_bitcast_fusion.2, s32[1024]{0:T(1024)S(1)} %pad_clamp_fusion.4), kind=kCustom, calls=%fused_computation.1.clone.1 | custom fusion | bytes 31457600 | tf_op jit(solution)/shard_map/while/body/eval_jaxpr/jit(_take)/gather | solution.py:74
  223.1 8.0 %fusion.30 = f32[8,3,2,16,256]{4,3,2,1,0:T(8,128)S(1)} fusion(bf16[8,10,3,128,256]{4,3,2,1,0:T(8,128)(2,1)} %bitcast.98, pred[8,10]{1,0:T(8,128)(4,1)S(1)} %copy-done.6, bf16[8,10,3,2,16,128]{5,4,3,2,1,0:T(8,128)(2,1)} %bitcast.99, pred[8,10]{1,0:T(8,128)(4,1)S(1)} %copy-done.7, bf16[8,10]{1,0:T(8,128)(2,1)S(1)} %fusion.29), kind=kOutput, calls=%fused_computation.8.clone.1 | convolution fusion | flops 513146880 | bytes 18481472 | tf_op jit(solution)/shard_map/while/body/eval_jaxpr/fsarkt,frktc->rfsac/dot_general | solution.py:75
  232.9 6.7 %collective-permute-start = (bf16[3,2,16,1024]{3,2,1,0:T(8,128)(2,1)S(1)}, bf16[3,2,16,1024]{3,2,1,0:T(8,128)(2,1)S(1)}, u32[]{:S(2)}, u32[]{:S(2)}) collective-permute-start(bf16[3,2,16,1024]{3,2,1,0:T(8,128)(2,1)S(1)} %get-tuple-element.365), channel_id=1, source_target_pairs={{2,0},{4,2},{6,4},{8,6},{10,8},{12,10},{14,12},{16,14},{18,16},{20... | collective-permute-start | bytes 589832 | tf_op jit(solution)/shard_map/while/body/eval_jaxpr/ppermute | solution.py:19
  247.2 8.2 %gather_fusion = bf16[80,3,128,256]{3,2,1,0:T(8,128)(2,1)} fusion(bf16[3,8,128,256]{3,2,1,0:T(8,128)(2,1)S(1)} %dynamic-slice_bitcast_fusion.2, s32[1024]{0:T(1024)S(1)} %pad_clamp_fusion.4), kind=kCustom, calls=%fused_computation.1.clone.1 | custom fusion | bytes 31457600 | tf_op jit(solution)/shard_map/while/body/eval_jaxpr/jit(_take)/gather | solution.py:74
  259.5 8.0 %fusion.30 = f32[8,3,2,16,256]{4,3,2,1,0:T(8,128)S(1)} fusion(bf16[8,10,3,128,256]{4,3,2,1,0:T(8,128)(2,1)} %bitcast.98, pred[8,10]{1,0:T(8,128)(4,1)S(1)} %copy-done.6, bf16[8,10,3,2,16,128]{5,4,3,2,1,0:T(8,128)(2,1)} %bitcast.99, pred[8,10]{1,0:T(8,128)(4,1)S(1)} %copy-done.7, bf16[8,10]{1,0:T(8,128)(2,1)S(1)} %fusion.29), kind=kOutput, calls=%fused_computation.8.clone.1 | convolution fusion | flops 513146880 | bytes 18481472 | tf_op jit(solution)/shard_map/while/body/eval_jaxpr/fsarkt,frktc->rfsac/dot_general | solution.py:75
  269.2 6.7 %collective-permute-start = (bf16[3,2,16,1024]{3,2,1,0:T(8,128)(2,1)S(1)}, bf16[3,2,16,1024]{3,2,1,0:T(8,128)(2,1)S(1)}, u32[]{:S(2)}, u32[]{:S(2)}) collective-permute-start(bf16[3,2,16,1024]{3,2,1,0:T(8,128)(2,1)S(1)} %get-tuple-element.365), channel_id=1, source_target_pairs={{2,0},{4,2},{6,4},{8,6},{10,8},{12,10},{14,12},{16,14},{18,16},{20... | collective-permute-start | bytes 589832 | tf_op jit(solution)/shard_map/while/body/eval_jaxpr/ppermute | solution.py:19
  283.5 8.1 %gather_fusion = bf16[80,3,128,256]{3,2,1,0:T(8,128)(2,1)} fusion(bf16[3,8,128,256]{3,2,1,0:T(8,128)(2,1)S(1)} %dynamic-slice_bitcast_fusion.2, s32[1024]{0:T(1024)S(1)} %pad_clamp_fusion.4), kind=kCustom, calls=%fused_computation.1.clone.1 | custom fusion | bytes 31457600 | tf_op jit(solution)/shard_map/while/body/eval_jaxpr/jit(_take)/gather | solution.py:74
  295.8 8.0 %fusion.30 = f32[8,3,2,16,256]{4,3,2,1,0:T(8,128)S(1)} fusion(bf16[8,10,3,128,256]{4,3,2,1,0:T(8,128)(2,1)} %bitcast.98, pred[8,10]{1,0:T(8,128)(4,1)S(1)} %copy-done.6, bf16[8,10,3,2,16,128]{5,4,3,2,1,0:T(8,128)(2,1)} %bitcast.99, pred[8,10]{1,0:T(8,128)(4,1)S(1)} %copy-done.7, bf16[8,10]{1,0:T(8,128)(2,1)S(1)} %fusion.29), kind=kOutput, calls=%fused_computation.8.clone.1 | convolution fusion | flops 513146880 | bytes 18481472 | tf_op jit(solution)/shard_map/while/body/eval_jaxpr/fsarkt,frktc->rfsac/dot_general | solution.py:75
  305.5 6.7 %collective-permute-start = (bf16[3,2,16,1024]{3,2,1,0:T(8,128)(2,1)S(1)}, bf16[3,2,16,1024]{3,2,1,0:T(8,128)(2,1)S(1)}, u32[]{:S(2)}, u32[]{:S(2)}) collective-permute-start(bf16[3,2,16,1024]{3,2,1,0:T(8,128)(2,1)S(1)} %get-tuple-element.365), channel_id=1, source_target_pairs={{2,0},{4,2},{6,4},{8,6},{10,8},{12,10},{14,12},{16,14},{18,16},{20... | collective-permute-start | bytes 589832 | tf_op jit(solution)/shard_map/while/body/eval_jaxpr/ppermute | solution.py:19
  319.9 8.2 %gather_fusion = bf16[80,3,128,256]{3,2,1,0:T(8,128)(2,1)} fusion(bf16[3,8,128,256]{3,2,1,0:T(8,128)(2,1)S(1)} %dynamic-slice_bitcast_fusion.2, s32[1024]{0:T(1024)S(1)} %pad_clamp_fusion.4), kind=kCustom, calls=%fused_computation.1.clone.1 | custom fusion | bytes 31457600 | tf_op jit(solution)/shard_map/while/body/eval_jaxpr/jit(_take)/gather | solution.py:74
  332.2 8.0 %fusion.30 = f32[8,3,2,16,256]{4,3,2,1,0:T(8,128)S(1)} fusion(bf16[8,10,3,128,256]{4,3,2,1,0:T(8,128)(2,1)} %bitcast.98, pred[8,10]{1,0:T(8,128)(4,1)S(1)} %copy-done.6, bf16[8,10,3,2,16,128]{5,4,3,2,1,0:T(8,128)(2,1)} %bitcast.99, pred[8,10]{1,0:T(8,128)(4,1)S(1)} %copy-done.7, bf16[8,10]{1,0:T(8,128)(2,1)S(1)} %fusion.29), kind=kOutput, calls=%fused_computation.8.clone.1 | convolution fusion | flops 513146880 | bytes 18481472 | tf_op jit(solution)/shard_map/while/body/eval_jaxpr/fsarkt,frktc->rfsac/dot_general | solution.py:75
  342.0 6.7 %collective-permute-start = (bf16[3,2,16,1024]{3,2,1,0:T(8,128)(2,1)S(1)}, bf16[3,2,16,1024]{3,2,1,0:T(8,128)(2,1)S(1)}, u32[]{:S(2)}, u32[]{:S(2)}) collective-permute-start(bf16[3,2,16,1024]{3,2,1,0:T(8,128)(2,1)S(1)} %get-tuple-element.365), channel_id=1, source_target_pairs={{2,0},{4,2},{6,4},{8,6},{10,8},{12,10},{14,12},{16,14},{18,16},{20... | collective-permute-start | bytes 589832 | tf_op jit(solution)/shard_map/while/body/eval_jaxpr/ppermute | solution.py:19
  356.2 8.1 %gather_fusion = bf16[80,3,128,256]{3,2,1,0:T(8,128)(2,1)} fusion(bf16[3,8,128,256]{3,2,1,0:T(8,128)(2,1)S(1)} %dynamic-slice_bitcast_fusion.2, s32[1024]{0:T(1024)S(1)} %pad_clamp_fusion.4), kind=kCustom, calls=%fused_computation.1.clone.1 | custom fusion | bytes 31457600 | tf_op jit(solution)/shard_map/while/body/eval_jaxpr/jit(_take)/gather | solution.py:74
  368.5 8.0 %fusion.30 = f32[8,3,2,16,256]{4,3,2,1,0:T(8,128)S(1)} fusion(bf16[8,10,3,128,256]{4,3,2,1,0:T(8,128)(2,1)} %bitcast.98, pred[8,10]{1,0:T(8,128)(4,1)S(1)} %copy-done.6, bf16[8,10,3,2,16,128]{5,4,3,2,1,0:T(8,128)(2,1)} %bitcast.99, pred[8,10]{1,0:T(8,128)(4,1)S(1)} %copy-done.7, bf16[8,10]{1,0:T(8,128)(2,1)S(1)} %fusion.29), kind=kOutput, calls=%fused_computation.8.clone.1 | convolution fusion | flops 513146880 | bytes 18481472 | tf_op jit(solution)/shard_map/while/body/eval_jaxpr/fsarkt,frktc->rfsac/dot_general | solution.py:75
  378.2 6.7 %collective-permute-start = (bf16[3,2,16,1024]{3,2,1,0:T(8,128)(2,1)S(1)}, bf16[3,2,16,1024]{3,2,1,0:T(8,128)(2,1)S(1)}, u32[]{:S(2)}, u32[]{:S(2)}) collective-permute-start(bf16[3,2,16,1024]{3,2,1,0:T(8,128)(2,1)S(1)} %get-tuple-element.365), channel_id=1, source_target_pairs={{2,0},{4,2},{6,4},{8,6},{10,8},{12,10},{14,12},{16,14},{18,16},{20... | collective-permute-start | bytes 589832 | tf_op jit(solution)/shard_map/while/body/eval_jaxpr/ppermute | solution.py:19
  392.5 8.2 %gather_fusion = bf16[80,3,128,256]{3,2,1,0:T(8,128)(2,1)} fusion(bf16[3,8,128,256]{3,2,1,0:T(8,128)(2,1)S(1)} %dynamic-slice_bitcast_fusion.2, s32[1024]{0:T(1024)S(1)} %pad_clamp_fusion.4), kind=kCustom, calls=%fused_computation.1.clone.1 | custom fusion | bytes 31457600 | tf_op jit(solution)/shard_map/while/body/eval_jaxpr/jit(_take)/gather | solution.py:74
  404.9 8.0 %fusion.30 = f32[8,3,2,16,256]{4,3,2,1,0:T(8,128)S(1)} fusion(bf16[8,10,3,128,256]{4,3,2,1,0:T(8,128)(2,1)} %bitcast.98, pred[8,10]{1,0:T(8,128)(4,1)S(1)} %copy-done.6, bf16[8,10,3,2,16,128]{5,4,3,2,1,0:T(8,128)(2,1)} %bitcast.99, pred[8,10]{1,0:T(8,128)(4,1)S(1)} %copy-done.7, bf16[8,10]{1,0:T(8,128)(2,1)S(1)} %fusion.29), kind=kOutput, calls=%fused_computation.8.clone.1 | convolution fusion | flops 513146880 | bytes 18481472 | tf_op jit(solution)/shard_map/while/body/eval_jaxpr/fsarkt,frktc->rfsac/dot_general | solution.py:75
  414.6 6.6 %collective-permute-start = (bf16[3,2,16,1024]{3,2,1,0:T(8,128)(2,1)S(1)}, bf16[3,2,16,1024]{3,2,1,0:T(8,128)(2,1)S(1)}, u32[]{:S(2)}, u32[]{:S(2)}) collective-permute-start(bf16[3,2,16,1024]{3,2,1,0:T(8,128)(2,1)S(1)} %get-tuple-element.365), channel_id=1, source_target_pairs={{2,0},{4,2},{6,4},{8,6},{10,8},{12,10},{14,12},{16,14},{18,16},{20... | collective-permute-start | bytes 589832 | tf_op jit(solution)/shard_map/while/body/eval_jaxpr/ppermute | solution.py:19
  428.8 8.2 %gather_fusion = bf16[80,3,128,256]{3,2,1,0:T(8,128)(2,1)} fusion(bf16[3,8,128,256]{3,2,1,0:T(8,128)(2,1)S(1)} %dynamic-slice_bitcast_fusion.2, s32[1024]{0:T(1024)S(1)} %pad_clamp_fusion.4), kind=kCustom, calls=%fused_computation.1.clone.1 | custom fusion | bytes 31457600 | tf_op jit(solution)/shard_map/while/body/eval_jaxpr/jit(_take)/gather | solution.py:74
  441.1 8.0 %fusion.30 = f32[8,3,2,16,256]{4,3,2,1,0:T(8,128)S(1)} fusion(bf16[8,10,3,128,256]{4,3,2,1,0:T(8,128)(2,1)} %bitcast.98, pred[8,10]{1,0:T(8,128)(4,1)S(1)} %copy-done.6, bf16[8,10,3,2,16,128]{5,4,3,2,1,0:T(8,128)(2,1)} %bitcast.99, pred[8,10]{1,0:T(8,128)(4,1)S(1)} %copy-done.7, bf16[8,10]{1,0:T(8,128)(2,1)S(1)} %fusion.29), kind=kOutput, calls=%fused_computation.8.clone.1 | convolution fusion | flops 513146880 | bytes 18481472 | tf_op jit(solution)/shard_map/while/body/eval_jaxpr/fsarkt,frktc->rfsac/dot_general | solution.py:75
  450.9 6.7 %collective-permute-start = (bf16[3,2,16,1024]{3,2,1,0:T(8,128)(2,1)S(1)}, bf16[3,2,16,1024]{3,2,1,0:T(8,128)(2,1)S(1)}, u32[]{:S(2)}, u32[]{:S(2)}) collective-permute-start(bf16[3,2,16,1024]{3,2,1,0:T(8,128)(2,1)S(1)} %get-tuple-element.365), channel_id=1, source_target_pairs={{2,0},{4,2},{6,4},{8,6},{10,8},{12,10},{14,12},{16,14},{18,16},{20... | collective-permute-start | bytes 589832 | tf_op jit(solution)/shard_map/while/body/eval_jaxpr/ppermute | solution.py:19
  465.1 8.1 %gather_fusion = bf16[80,3,128,256]{3,2,1,0:T(8,128)(2,1)} fusion(bf16[3,8,128,256]{3,2,1,0:T(8,128)(2,1)S(1)} %dynamic-slice_bitcast_fusion.2, s32[1024]{0:T(1024)S(1)} %pad_clamp_fusion.4), kind=kCustom, calls=%fused_computation.1.clone.1 | custom fusion | bytes 31457600 | tf_op jit(solution)/shard_map/while/body/eval_jaxpr/jit(_take)/gather | solution.py:74
  477.4 8.0 %fusion.30 = f32[8,3,2,16,256]{4,3,2,1,0:T(8,128)S(1)} fusion(bf16[8,10,3,128,256]{4,3,2,1,0:T(8,128)(2,1)} %bitcast.98, pred[8,10]{1,0:T(8,128)(4,1)S(1)} %copy-done.6, bf16[8,10,3,2,16,128]{5,4,3,2,1,0:T(8,128)(2,1)} %bitcast.99, pred[8,10]{1,0:T(8,128)(4,1)S(1)} %copy-done.7, bf16[8,10]{1,0:T(8,128)(2,1)S(1)} %fusion.29), kind=kOutput, calls=%fused_computation.8.clone.1 | convolution fusion | flops 513146880 | bytes 18481472 | tf_op jit(solution)/shard_map/while/body/eval_jaxpr/fsarkt,frktc->rfsac/dot_general | solution.py:75
  488.0 11.5 %all_to_all.10 = f32[8,1,1024]{2,1,0:T(1,128)S(1)} all-to-all(f32[8,1,1024]{2,1,0:T(1,128)S(1)} %reshape.218), channel_id=1, replica_groups=mesh['depth'=8,'lat'=32,'freq'=2] {'depth'}, dimensions={0} | all-to-all | bytes 65536 | tf_op jit(solution)/shard_map/all_to_all | solution.py:58
  499.5 17.5 %psum.7 = f32[1024]{0:T(1024)S(1)} all-reduce(f32[1024]{0:T(1024)S(1)} %reduce_sum.20), channel_id=1, replica_groups=mesh['depth'=8,'lat'=32,'freq'=2] {'freq'}, use_global_device_ids=true, to_apply=%region_4.5 | all-reduce | flops 1024 | bytes 8192 | tf_op jit(solution)/shard_map/psum | solution.py:136
  (229 shorter events, 162.7 us)
Async XLA Ops:
  0.0 173.7 %copy-start = (bf16[3,2,128,1024]{3,2,1,0:T(8,128)(2,1)S(1)}, bf16[3,2,128,1024]{3,2,1,0:T(8,128)(2,1)}, u32[]{:S(2)}) copy-start(bf16[3,2,128,1024]{3,2,1,0:T(8,128)(2,1)} %param.8) | copy-start | bytes 4718596
  0.0 35.2 %collective-permute-start.2 = (bf16[1,3,8,128,256]{4,3,2,1,0:T(8,128)(2,1)}, bf16[1,3,8,128,256]{4,3,2,1,0:T(8,128)(2,1)S(1)}, u32[]{:S(2)}, u32[]{:S(2)}) collective-permute-start(bf16[1,3,8,128,256]{4,3,2,1,0:T(8,128)(2,1)} %param.10), channel_id=1, source_target_pairs={{0,64},{64,128},{128,192},{192,256},{256,320},{320,384},{384,448},... | collective-permute-start | bytes 4718600 | tf_op jit(solution)/shard_map/ppermute | solution.py:105
  4.2 36.8 %collective-permute-start.3 = (bf16[1,3,8,128,256]{4,3,2,1,0:T(8,128)(2,1)}, bf16[1,3,8,128,256]{4,3,2,1,0:T(8,128)(2,1)S(1)}, u32[]{:S(2)}, u32[]{:S(2)}) collective-permute-start(bf16[1,3,8,128,256]{4,3,2,1,0:T(8,128)(2,1)} %param.10), channel_id=1, source_target_pairs={{0,448},{64,0},{128,64},{192,128},{256,192},{320,256},{384,320},{4... | collective-permute-start | bytes 4718600 | tf_op jit(solution)/shard_map/ppermute | solution.py:110
  35.2 39.9 %collective-permute-start.4 = (bf16[1,3,8,128,256]{4,3,2,1,0:T(8,128)(2,1)S(1)}, bf16[1,3,8,128,256]{4,3,2,1,0:T(8,128)(2,1)S(1)}, u32[]{:S(2)}, u32[]{:S(2)}) collective-permute-start(bf16[1,3,8,128,256]{4,3,2,1,0:T(8,128)(2,1)S(1)} %collective-permute-done.2), channel_id=1, source_target_pairs={{0,64},{64,128},{128,192},{192,256},{256,320},{320,384},{384,448},... | collective-permute-start | bytes 4718600 | tf_op jit(solution)/shard_map/ppermute | solution.py:105
  41.0 34.1 %copy-start.2 = (bf16[1,3,8,128,256]{4,3,2,1,0:T(8,128)(2,1)}, bf16[1,3,8,128,256]{4,3,2,1,0:T(8,128)(2,1)S(1)}, u32[]{:S(2)}) copy-start(bf16[1,3,8,128,256]{4,3,2,1,0:T(8,128)(2,1)S(1)} %collective-permute-done.3) | copy-start | bytes 4718596
  41.0 36.6 %collective-permute-start.5 = (bf16[1,3,8,128,256]{4,3,2,1,0:T(8,128)(2,1)S(1)}, bf16[1,3,8,128,256]{4,3,2,1,0:T(8,128)(2,1)}, u32[]{:S(2)}, u32[]{:S(2)}) collective-permute-start(bf16[1,3,8,128,256]{4,3,2,1,0:T(8,128)(2,1)S(1)} %collective-permute-done.3), channel_id=1, source_target_pairs={{0,448},{64,0},{128,64},{192,128},{256,192},{320,256},{384,320},{4... | collective-permute-start | bytes 4718600 | tf_op jit(solution)/shard_map/ppermute | solution.py:110
  75.1 2.5 copy-start.4
  75.1 35.6 %collective-permute-start.6 = (bf16[1,3,8,128,256]{4,3,2,1,0:T(8,128)(2,1)S(1)}, bf16[1,3,8,128,256]{4,3,2,1,0:T(8,128)(2,1)}, u32[]{:S(2)}, u32[]{:S(2)}) collective-permute-start(bf16[1,3,8,128,256]{4,3,2,1,0:T(8,128)(2,1)S(1)} %collective-permute-done.4), channel_id=1, source_target_pairs={{0,64},{64,128},{128,192},{192,256},{256,320},{320,384},{384,448},... | collective-permute-start | bytes 4718600 | tf_op jit(solution)/shard_map/ppermute | solution.py:105
  77.6 107.0 %collective-permute-start.7 = (bf16[1,3,8,128,256]{4,3,2,1,0:T(8,128)(2,1)}, bf16[1,3,8,128,256]{4,3,2,1,0:T(8,128)(2,1)}, u32[]{:S(2)}, u32[]{:S(2)}) collective-permute-start(bf16[1,3,8,128,256]{4,3,2,1,0:T(8,128)(2,1)} %collective-permute-done.5), channel_id=1, source_target_pairs={{0,448},{64,0},{128,64},{192,128},{256,192},{320,256},{384,320},{4... | collective-permute-start | bytes 4718600 | tf_op jit(solution)/shard_map/ppermute | solution.py:110
  110.7 76.6 %collective-permute-start.8 = (bf16[1,3,8,128,256]{4,3,2,1,0:T(8,128)(2,1)}, bf16[1,3,8,128,256]{4,3,2,1,0:T(8,128)(2,1)}, u32[]{:S(2)}, u32[]{:S(2)}) collective-permute-start(bf16[1,3,8,128,256]{4,3,2,1,0:T(8,128)(2,1)} %collective-permute-done.6), channel_id=1, source_target_pairs={{0,64},{64,128},{128,192},{192,256},{256,320},{320,384},{384,448},... | collective-permute-start | bytes 4718600 | tf_op jit(solution)/shard_map/ppermute | solution.py:105
  114.2 60.4 %all-to-all-start = ((f32[8,1,1024]{2,1,0:T(1,128)}), f32[8,1,1024]{2,1,0:T(1,128)S(1)}, u32[]{:S(2)}, u32[]{:S(2)}) async-start(f32[8,1,1024]{2,1,0:T(1,128)} %broadcast_in_dim.92), calls=%async_computation | async-start | bytes 65536 | tf_op jit(solution)/shard_map/all_to_all | solution.py:37
  165.6 6.2 %copy-start.1 = (bf16[1,3,8,128,256]{4,3,2,1,0:T(8,128)(2,1)S(1)}, bf16[1,3,8,128,256]{4,3,2,1,0:T(8,128)(2,1)}, u32[]{:S(2)}) copy-start(bf16[1,3,8,128,256]{4,3,2,1,0:T(8,128)(2,1)} %param.10) | copy-start | bytes 4718596
  175.3 2.5 copy-start.5
  190.1 29.6 %collective-permute-start = (bf16[3,2,16,1024]{3,2,1,0:T(8,128)(2,1)S(1)}, bf16[3,2,16,1024]{3,2,1,0:T(8,128)(2,1)S(1)}, u32[]{:S(2)}, u32[]{:S(2)}) collective-permute-start(bf16[3,2,16,1024]{3,2,1,0:T(8,128)(2,1)S(1)} %get-tuple-element.365), channel_id=1, source_target_pairs={{2,0},{4,2},{6,4},{8,6},{10,8},{12,10},{14,12},{16,14},{18,16},{20... | collective-permute-start | bytes 589832 | tf_op jit(solution)/shard_map/while/body/eval_jaxpr/ppermute | solution.py:19
  203.2 16.4 %collective-permute-start.1 = (bf16[3,2,16,1024]{3,2,1,0:T(8,128)(2,1)S(1)}, bf16[3,2,16,1024]{3,2,1,0:T(8,128)(2,1)}, u32[]{:S(2)}, u32[]{:S(2)}) collective-permute-start(bf16[3,2,16,1024]{3,2,1,0:T(8,128)(2,1)S(1)} %get-tuple-element.365), channel_id=1, source_target_pairs={{0,2},{2,4},{4,6},{6,8},{8,10},{10,12},{12,14},{14,16},{16,18},{18... | collective-permute-start | bytes 589832 | tf_op jit(solution)/shard_map/while/body/eval_jaxpr/ppermute | solution.py:16
  232.9 23.1 %collective-permute-start = (bf16[3,2,16,1024]{3,2,1,0:T(8,128)(2,1)S(1)}, bf16[3,2,16,1024]{3,2,1,0:T(8,128)(2,1)S(1)}, u32[]{:S(2)}, u32[]{:S(2)}) collective-permute-start(bf16[3,2,16,1024]{3,2,1,0:T(8,128)(2,1)S(1)} %get-tuple-element.365), channel_id=1, source_target_pairs={{2,0},{4,2},{6,4},{8,6},{10,8},{12,10},{14,12},{16,14},{18,16},{20... | collective-permute-start | bytes 589832 | tf_op jit(solution)/shard_map/while/body/eval_jaxpr/ppermute | solution.py:19
  239.6 16.4 %collective-permute-start.1 = (bf16[3,2,16,1024]{3,2,1,0:T(8,128)(2,1)S(1)}, bf16[3,2,16,1024]{3,2,1,0:T(8,128)(2,1)}, u32[]{:S(2)}, u32[]{:S(2)}) collective-permute-start(bf16[3,2,16,1024]{3,2,1,0:T(8,128)(2,1)S(1)} %get-tuple-element.365), channel_id=1, source_target_pairs={{0,2},{2,4},{4,6},{6,8},{8,10},{10,12},{12,14},{14,16},{16,18},{18... | collective-permute-start | bytes 589832 | tf_op jit(solution)/shard_map/while/body/eval_jaxpr/ppermute | solution.py:16
  269.2 23.1 %collective-permute-start = (bf16[3,2,16,1024]{3,2,1,0:T(8,128)(2,1)S(1)}, bf16[3,2,16,1024]{3,2,1,0:T(8,128)(2,1)S(1)}, u32[]{:S(2)}, u32[]{:S(2)}) collective-permute-start(bf16[3,2,16,1024]{3,2,1,0:T(8,128)(2,1)S(1)} %get-tuple-element.365), channel_id=1, source_target_pairs={{2,0},{4,2},{6,4},{8,6},{10,8},{12,10},{14,12},{16,14},{18,16},{20... | collective-permute-start | bytes 589832 | tf_op jit(solution)/shard_map/while/body/eval_jaxpr/ppermute | solution.py:19
  275.9 16.4 %collective-permute-start.1 = (bf16[3,2,16,1024]{3,2,1,0:T(8,128)(2,1)S(1)}, bf16[3,2,16,1024]{3,2,1,0:T(8,128)(2,1)}, u32[]{:S(2)}, u32[]{:S(2)}) collective-permute-start(bf16[3,2,16,1024]{3,2,1,0:T(8,128)(2,1)S(1)} %get-tuple-element.365), channel_id=1, source_target_pairs={{0,2},{2,4},{4,6},{6,8},{8,10},{10,12},{12,14},{14,16},{16,18},{18... | collective-permute-start | bytes 589832 | tf_op jit(solution)/shard_map/while/body/eval_jaxpr/ppermute | solution.py:16
  293.3 2.4 copy-start.6
  305.5 23.2 %collective-permute-start = (bf16[3,2,16,1024]{3,2,1,0:T(8,128)(2,1)S(1)}, bf16[3,2,16,1024]{3,2,1,0:T(8,128)(2,1)S(1)}, u32[]{:S(2)}, u32[]{:S(2)}) collective-permute-start(bf16[3,2,16,1024]{3,2,1,0:T(8,128)(2,1)S(1)} %get-tuple-element.365), channel_id=1, source_target_pairs={{2,0},{4,2},{6,4},{8,6},{10,8},{12,10},{14,12},{16,14},{18,16},{20... | collective-permute-start | bytes 589832 | tf_op jit(solution)/shard_map/while/body/eval_jaxpr/ppermute | solution.py:19
  312.3 16.4 %collective-permute-start.1 = (bf16[3,2,16,1024]{3,2,1,0:T(8,128)(2,1)S(1)}, bf16[3,2,16,1024]{3,2,1,0:T(8,128)(2,1)}, u32[]{:S(2)}, u32[]{:S(2)}) collective-permute-start(bf16[3,2,16,1024]{3,2,1,0:T(8,128)(2,1)S(1)} %get-tuple-element.365), channel_id=1, source_target_pairs={{0,2},{2,4},{4,6},{6,8},{8,10},{10,12},{12,14},{14,16},{16,18},{18... | collective-permute-start | bytes 589832 | tf_op jit(solution)/shard_map/while/body/eval_jaxpr/ppermute | solution.py:16
  342.0 23.1 %collective-permute-start = (bf16[3,2,16,1024]{3,2,1,0:T(8,128)(2,1)S(1)}, bf16[3,2,16,1024]{3,2,1,0:T(8,128)(2,1)S(1)}, u32[]{:S(2)}, u32[]{:S(2)}) collective-permute-start(bf16[3,2,16,1024]{3,2,1,0:T(8,128)(2,1)S(1)} %get-tuple-element.365), channel_id=1, source_target_pairs={{2,0},{4,2},{6,4},{8,6},{10,8},{12,10},{14,12},{16,14},{18,16},{20... | collective-permute-start | bytes 589832 | tf_op jit(solution)/shard_map/while/body/eval_jaxpr/ppermute | solution.py:19
  348.6 16.4 %collective-permute-start.1 = (bf16[3,2,16,1024]{3,2,1,0:T(8,128)(2,1)S(1)}, bf16[3,2,16,1024]{3,2,1,0:T(8,128)(2,1)}, u32[]{:S(2)}, u32[]{:S(2)}) collective-permute-start(bf16[3,2,16,1024]{3,2,1,0:T(8,128)(2,1)S(1)} %get-tuple-element.365), channel_id=1, source_target_pairs={{0,2},{2,4},{4,6},{6,8},{8,10},{10,12},{12,14},{14,16},{16,18},{18... | collective-permute-start | bytes 589832 | tf_op jit(solution)/shard_map/while/body/eval_jaxpr/ppermute | solution.py:16
  366.0 2.4 copy-start.6
  378.2 23.2 %collective-permute-start = (bf16[3,2,16,1024]{3,2,1,0:T(8,128)(2,1)S(1)}, bf16[3,2,16,1024]{3,2,1,0:T(8,128)(2,1)S(1)}, u32[]{:S(2)}, u32[]{:S(2)}) collective-permute-start(bf16[3,2,16,1024]{3,2,1,0:T(8,128)(2,1)S(1)} %get-tuple-element.365), channel_id=1, source_target_pairs={{2,0},{4,2},{6,4},{8,6},{10,8},{12,10},{14,12},{16,14},{18,16},{20... | collective-permute-start | bytes 589832 | tf_op jit(solution)/shard_map/while/body/eval_jaxpr/ppermute | solution.py:19
  385.0 16.5 %collective-permute-start.1 = (bf16[3,2,16,1024]{3,2,1,0:T(8,128)(2,1)S(1)}, bf16[3,2,16,1024]{3,2,1,0:T(8,128)(2,1)}, u32[]{:S(2)}, u32[]{:S(2)}) collective-permute-start(bf16[3,2,16,1024]{3,2,1,0:T(8,128)(2,1)S(1)} %get-tuple-element.365), channel_id=1, source_target_pairs={{0,2},{2,4},{4,6},{6,8},{8,10},{10,12},{12,14},{14,16},{16,18},{18... | collective-permute-start | bytes 589832 | tf_op jit(solution)/shard_map/while/body/eval_jaxpr/ppermute | solution.py:16
  414.6 23.0 %collective-permute-start = (bf16[3,2,16,1024]{3,2,1,0:T(8,128)(2,1)S(1)}, bf16[3,2,16,1024]{3,2,1,0:T(8,128)(2,1)S(1)}, u32[]{:S(2)}, u32[]{:S(2)}) collective-permute-start(bf16[3,2,16,1024]{3,2,1,0:T(8,128)(2,1)S(1)} %get-tuple-element.365), channel_id=1, source_target_pairs={{2,0},{4,2},{6,4},{8,6},{10,8},{12,10},{14,12},{16,14},{18,16},{20... | collective-permute-start | bytes 589832 | tf_op jit(solution)/shard_map/while/body/eval_jaxpr/ppermute | solution.py:19
  421.2 16.4 %collective-permute-start.1 = (bf16[3,2,16,1024]{3,2,1,0:T(8,128)(2,1)S(1)}, bf16[3,2,16,1024]{3,2,1,0:T(8,128)(2,1)}, u32[]{:S(2)}, u32[]{:S(2)}) collective-permute-start(bf16[3,2,16,1024]{3,2,1,0:T(8,128)(2,1)S(1)} %get-tuple-element.365), channel_id=1, source_target_pairs={{0,2},{2,4},{4,6},{6,8},{8,10},{10,12},{12,14},{14,16},{16,18},{18... | collective-permute-start | bytes 589832 | tf_op jit(solution)/shard_map/while/body/eval_jaxpr/ppermute | solution.py:16
  438.7 2.4 copy-start.6
  450.9 23.1 %collective-permute-start = (bf16[3,2,16,1024]{3,2,1,0:T(8,128)(2,1)S(1)}, bf16[3,2,16,1024]{3,2,1,0:T(8,128)(2,1)S(1)}, u32[]{:S(2)}, u32[]{:S(2)}) collective-permute-start(bf16[3,2,16,1024]{3,2,1,0:T(8,128)(2,1)S(1)} %get-tuple-element.365), channel_id=1, source_target_pairs={{2,0},{4,2},{6,4},{8,6},{10,8},{12,10},{14,12},{16,14},{18,16},{20... | collective-permute-start | bytes 589832 | tf_op jit(solution)/shard_map/while/body/eval_jaxpr/ppermute | solution.py:19
  457.6 16.4 %collective-permute-start.1 = (bf16[3,2,16,1024]{3,2,1,0:T(8,128)(2,1)S(1)}, bf16[3,2,16,1024]{3,2,1,0:T(8,128)(2,1)}, u32[]{:S(2)}, u32[]{:S(2)}) collective-permute-start(bf16[3,2,16,1024]{3,2,1,0:T(8,128)(2,1)S(1)} %get-tuple-element.365), channel_id=1, source_target_pairs={{0,2},{2,4},{4,6},{6,8},{8,10},{10,12},{12,14},{14,16},{16,18},{18... | collective-permute-start | bytes 589832 | tf_op jit(solution)/shard_map/while/body/eval_jaxpr/ppermute | solution.py:16
  (14 other events, 33.5 us)
